TPU v7x, 32 devices: a whole 2x2x4 slice. The times are simulated.
32 devices in a mesh: parts: 2 (over y), tensor: 4 (over z), section: 2 (over x), rows: 2 (over core).
Axes of the slice: x: 2, y: 2, z: 4, core: 2. Of those that a mesh axis runs over, the one named last changes fastest.
Arguments:
- tokens: bfloat16 [96, 8192], P('parts', ('tensor', 'rows')), parts along dimension 0, may hold values from -6 to 6
- gain: float32 [2, 8192], P('section'), may hold values from 0.1 to 1.9
- base_weight: bfloat16 [2, 8192, 8192], P('section', None, ('tensor', 'rows')), may hold values from -0.0625 to 0.0625
- down_weight_slots: bfloat16 [2, 4, 32, 8192], P('section', 'tensor', None, 'rows'), may hold values from -0.0625 to 0.0625
- up_weight_slots: bfloat16 [2, 4, 32, 8192], P('section', 'tensor', None, 'rows'), may hold values from -1 to 1
- row_adapter_index: int32 [96], P('parts'), parts along dimension 0, may hold values from 0 to 3
- adapter_slot_index: int32 [4], replicated, may hold values from 0 to 3, each once
Outputs:
- mixed: bfloat16 [96, 8192], P(('parts', 'section'), ('tensor', 'rows')), parts along dimension 0
There are 2 independent parts, one for each index of `parts`. A program takes and returns all parts, laid end to end along the dimension named above; an argument that names none is the same for every part. Nothing has to cross between parts.
Inputs may be any that keep to these rules, and one draw needn't show every extreme that they name: `adapter_slot_index`: each adapter's storage slot; every slot is used once.
All inputs are finite; a program needn't handle non-finite values.
Results may differ from a plain program's by a relative error of at most 0.0059.
Values may be sent and summed in bfloat16 or wider, within the bound.
A program may use at most 64 MiB of HBM per device.

v0:
```python
import jax
import jax.numpy as jnp
from jax import lax
from jax.sharding import PartitionSpec as P

epsilon = 1e-05


def passed_along(value, axis, steps):
    count = lax.axis_size(axis)
    initial, last = (max(0, -steps), min(count, count - steps))
    return lax.ppermute(value, axis, [(source, source + steps) for source in range(initial, last)])


def spread(x, axis, root):
    mine = lax.axis_index(axis) == root
    return lax.psum(jnp.where(mine, x, jnp.zeros_like(x)), axis)


def shards(
    tokens,
    gain,
    base_weight,
    down_weight_slots,
    up_weight_slots,
    row_adapter_index,
    adapter_slot_index,
):
    section_count = lax.axis_size("section")
    section_here = lax.axis_index("section")
    feature_block = lax.axis_index(("tensor", "rows"))
    half_here = lax.axis_index("rows")
    block_width = tokens.shape[1]
    all_rows = tokens.shape[0]
    slot_count = adapter_slot_index.shape[0]
    halves = (
        lax.all_gather(down_weight_slots, "rows", axis=3, tiled=True),
        lax.all_gather(up_weight_slots, "rows", axis=3, tiled=True),
    )
    blocks = (
        lax.all_to_all(halves[0], "tensor", split_axis=3, concat_axis=1, tiled=True),
        lax.all_to_all(halves[1], "tensor", split_axis=3, concat_axis=1, tiled=True),
    )
    down_block = lax.dynamic_slice_in_dim(blocks[0], half_here * block_width, block_width, 3)[0]
    up_block = lax.dynamic_slice_in_dim(blocks[1], half_here * block_width, block_width, 3)[0]
    slot_range = jnp.arange(slot_count, dtype=jnp.int32)
    id_match = (row_adapter_index[:, None] == slot_range[None, :]).astype(jnp.int32)
    slot_rows = jnp.sum(id_match * adapter_slot_index[None, :], axis=1)
    slot_hot = (slot_rows[:, None] == slot_range[None, :]).astype(jnp.float32)
    group_rows = all_rows // section_count
    tick_count = section_count + section_count - 1

    def apply_layer(inputs, row_hot):
        gathered = lax.all_gather(inputs, ("tensor", "rows"), axis=1, tiled=True)
        values = gathered.astype(jnp.float32)
        mean_square = jnp.mean(values * values, axis=1, keepdims=True)
        normalized_input = (values * gain[0] * lax.rsqrt(mean_square + epsilon)).astype(
            jnp.bfloat16
        )
        projected = jnp.dot(normalized_input, base_weight[0], preferred_element_type=jnp.float32)
        own_normed = lax.dynamic_slice_in_dim(
            normalized_input, feature_block * block_width, block_width, 1
        )
        rank_scores = jnp.einsum(
            "mw,krw->mkr", own_normed, down_block, preferred_element_type=jnp.float32
        )
        partial_value = jnp.sum(rank_scores * row_hot[:, :, None], axis=1)
        lowrank = lax.psum(partial_value, ("tensor", "rows")).astype(jnp.bfloat16)
        expanded_update = (row_hot[:, :, None] * lowrank.astype(jnp.float32)[:, None, :]).astype(
            jnp.bfloat16
        )
        adapter_update = jnp.einsum(
            "mkr,krw->mw", expanded_update, up_block, preferred_element_type=jnp.float32
        )
        return (inputs.astype(jnp.float32) + projected + 0.5 * adapter_update).astype(jnp.bfloat16)

    def one_tick(tick, carry):
        received, collected = carry
        group_index = tick - section_here
        active = (group_index >= 0) & (group_index < section_count)
        clipped = jnp.clip(group_index, 0, section_count - 1)
        first_rows = clipped * group_rows
        incoming = lax.dynamic_slice_in_dim(tokens, first_rows, group_rows, 0)
        layer_input = jnp.where(section_here == 0, incoming, received)
        row_hot = lax.dynamic_slice_in_dim(slot_hot, first_rows, group_rows, 0)
        outcome = apply_layer(layer_input, row_hot)
        store = active & (section_here == section_count - 1)
        previous = lax.dynamic_slice_in_dim(collected, first_rows, group_rows, 0)
        collected = lax.dynamic_update_slice_in_dim(
            collected, jnp.where(store, outcome, previous), first_rows, 0
        )
        received = passed_along(outcome, "section", 1)
        return (received, collected)

    start_rows = jnp.zeros((group_rows, block_width), jnp.bfloat16)
    start_store = jnp.zeros((all_rows, block_width), jnp.bfloat16)
    _, collected = lax.fori_loop(0, tick_count, one_tick, (start_rows, start_store))
    finished = spread(collected, "section", section_count - 1)
    share_rows = all_rows // section_count
    return lax.dynamic_slice_in_dim(finished, section_here * share_rows, share_rows, 0)


def solution(mesh):
    return jax.shard_map(
        shards,
        mesh=mesh,
        in_specs=(
            P("parts", ("tensor", "rows")),
            P("section", None),
            P("section", None, ("tensor", "rows")),
            P("section", "tensor", None, "rows"),
            P("section", "tensor", None, "rows"),
            P("parts"),
            P(),
        ),
        out_specs=P(("parts", "section"), ("tensor", "rows")),
        check_vma=False,
    )
```

profile of v0, /device:TPU:0, one launch (start us, length us, event | category | flops | bytes accessed | tf_op | source)
XLA Modules:
  0.0 356.9 jit_solution(12283347119068531822)
XLA Ops:
  6.5 2.5 all_gather.16
  9.0 6.7 %copy.24 = bf16[1,1,32,8192]{2,1,0,3:T(2,128)(2,1)} copy(bf16[1,1,32,8192]{3,2,1,0:T(8,128)(2,1)S(1)} %all_gather.16) | data formatting | bytes 1048576 | tf_op jit(solution)/shard_map/all_gather | solution.py:38
  16.2 45.3 %reduce = bf16[8192,32]{1,0:T(8,128)(2,1)S(1)} reduce(bf16[8192,1,1,32]{3,2,1,0:T(2,128)(2,1)} %bitcast.48, bf16[]{:T(256)} %broadcast.56), dimensions={1,2}, to_apply=%bitcast.31.reduce_sub_computation | reduce | bytes 1048578
  61.5 2.9 reshape.24
  64.4 6.2 %all-to-all-start.1 = ((bf16[4,2,32768]{2,1,0:T(2,128)(2,1)}), bf16[4,2,32768]{2,1,0:T(2,128)(2,1)S(1)}, u32[]{:S(2)}, u32[]{:S(2)}) async-start(bf16[4,2,32768]{2,1,0:T(2,128)(2,1)} %reshape.24), calls=%async_computation.1 | async-start | bytes 1048576 | tf_op jit(solution)/shard_map/all_to_all | solution.py:42
  70.6 2.3 all_gather.15
  73.0 6.7 %copy.22 = bf16[1,1,32,8192]{2,1,0,3:T(2,128)(2,1)} copy(bf16[1,1,32,8192]{3,2,1,0:T(8,128)(2,1)S(1)} %all_gather.15) | data formatting | bytes 1048576 | tf_op jit(solution)/shard_map/all_gather | solution.py:37
  79.7 45.2 %reduce.1 = bf16[8192,32]{1,0:T(8,128)(2,1)S(1)} reduce(bf16[8192,1,1,32]{3,2,1,0:T(2,128)(2,1)} %bitcast.49, bf16[]{:T(256)} %broadcast.56), dimensions={1,2}, to_apply=%bitcast.29.reduce_sub_computation | reduce | bytes 1048578
  124.9 2.9 reshape.22
  127.9 5.1 %all-to-all-start = ((bf16[4,2,32768]{2,1,0:T(2,128)(2,1)}), bf16[4,2,32768]{2,1,0:T(2,128)(2,1)S(1)}, u32[]{:S(2)}, u32[]{:S(2)}) async-start(bf16[4,2,32768]{2,1,0:T(2,128)(2,1)} %reshape.22), calls=%async_computation | async-start | bytes 1048576 | tf_op jit(solution)/shard_map/all_to_all | solution.py:41
  133.1 3.3 reshape.25
  136.4 8.0 %copy.25 = bf16[1,1,32,8192]{3,2,1,0:T(8,128)(2,1)S(1)} copy(bf16[1,1,32,8192]{2,1,0,3:T(2,128)(2,1)} %bitcast.50) | data formatting | bytes 1048576 | tf_op jit(solution)/shard_map/all_to_all | solution.py:42
  144.8 3.0 all-to-all-done
  147.8 3.3 reshape.23
  151.1 8.0 %copy.23 = bf16[1,1,32,8192]{3,2,1,0:T(8,128)(2,1)S(1)} copy(bf16[1,1,32,8192]{2,1,0,3:T(2,128)(2,1)} %bitcast.51) | data formatting | bytes 1048576 | tf_op jit(solution)/shard_map/all_to_all | solution.py:41
  159.9 167.8 %while.17 = (s32[]{:T(128)}, bf16[24,1024]{1,0:T(8,128)(2,1)S(1)}, bf16[48,1024]{1,0:T(8,128)(2,1)S(1)}, pred[]{:T(512)}, s32[]{:T(128)}, /*index=5*/bf16[48,102...) while((s32[]{:T(128)}, bf16[24,1024]{1,0:T(8,128)(2,1)S(1)}, ...), condition=%wide.region_5.6_spmd, body=%wide.region_1.5_spmd.sunk | while | flops 416797472 | bytes 20166088 | solution.py:97
  160.0 14.5 %all_gather.18 = bf16[24,8192]{1,0:T(8,128)(2,1)S(1)} all-gather(bf16[24,1024]{1,0:T(8,128)(2,1)S(1)} %dynamic-slice_select_fusion.2), channel_id=1, replica_groups=mesh['parts'=2,'tensor'=4,'section'=2,'rows'=2] {'tensor','rows'}, dimensions={1}, use_global_device_ids=true | all-gather | bytes 442368 | tf_op jit(solution)/shard_map/while/body/eval_jaxpr/all_gather | solution.py:54
  174.9 8.1 %fusion.37 = f32[24,1024]{1,0:T(8,128)S(1)} fusion(bf16[24,8192]{1,0:T(8,128)(2,1)S(1)} %fusion.36, bf16[1,8192,1024]{2,1,0:T(8,128)(2,1)} %get-tuple-element.482, bf16[24,1024]{1,0:T(8,128)(2,1)S(1)} %dynamic-slice_select_fusion.2), kind=kOutput, calls=%fused_computation.5.clone.1 | convolution fusion | flops 402702336 | bytes 17317888 | tf_op jit(solution)/shard_map/while/body/eval_jaxpr/dot_general | solution.py:60
  183.3 27.2 %psum.22 = bf16[24,32]{1,0:T(8,128)(2,1)S(1)} all-reduce(f32[24,32]{1,0:T(8,128)S(1)} %fusion.38), channel_id=1, replica_groups=mesh['parts'=2,'tensor'=4,'section'=2,'rows'=2] {'tensor','rows'}, use_global_device_ids=true, to_apply=%region_4.4 | all-reduce | flops 768 | bytes 4608 | tf_op jit(solution)/shard_map/while/body/eval_jaxpr/psum | solution.py:68
  210.8 3.4 collective-permute-start
  214.2 1.7 collective-permute-done
  215.9 14.5 %all_gather.18 = bf16[24,8192]{1,0:T(8,128)(2,1)S(1)} all-gather(bf16[24,1024]{1,0:T(8,128)(2,1)S(1)} %dynamic-slice_select_fusion.2), channel_id=1, replica_groups=mesh['parts'=2,'tensor'=4,'section'=2,'rows'=2] {'tensor','rows'}, dimensions={1}, use_global_device_ids=true | all-gather | bytes 442368 | tf_op jit(solution)/shard_map/while/body/eval_jaxpr/all_gather | solution.py:54
  230.8 8.1 %fusion.37 = f32[24,1024]{1,0:T(8,128)S(1)} fusion(bf16[24,8192]{1,0:T(8,128)(2,1)S(1)} %fusion.36, bf16[1,8192,1024]{2,1,0:T(8,128)(2,1)} %get-tuple-element.482, bf16[24,1024]{1,0:T(8,128)(2,1)S(1)} %dynamic-slice_select_fusion.2), kind=kOutput, calls=%fused_computation.5.clone.1 | convolution fusion | flops 402702336 | bytes 17317888 | tf_op jit(solution)/shard_map/while/body/eval_jaxpr/dot_general | solution.py:60
  239.2 26.4 %psum.22 = bf16[24,32]{1,0:T(8,128)(2,1)S(1)} all-reduce(f32[24,32]{1,0:T(8,128)S(1)} %fusion.38), channel_id=1, replica_groups=mesh['parts'=2,'tensor'=4,'section'=2,'rows'=2] {'tensor','rows'}, use_global_device_ids=true, to_apply=%region_4.4 | all-reduce | flops 768 | bytes 4608 | tf_op jit(solution)/shard_map/while/body/eval_jaxpr/psum | solution.py:68
  265.8 4.2 %collective-permute-start = (bf16[24,1024]{1,0:T(8,128)(2,1)S(1)}, bf16[24,1024]{1,0:T(8,128)(2,1)S(1)}, u32[]{:S(2)}, u32[]{:S(2)}) collective-permute-start(bf16[24,1024]{1,0:T(8,128)(2,1)S(1)} %get-tuple-element.437), channel_id=1, source_target_pairs={{0,2},{1,3},{4,6},{5,7},{8,10},{9,11},{12,14},{13,15},{16,18},{17,... | collective-permute-start | bytes 147464 | tf_op jit(solution)/shard_map/while/body/eval_jaxpr/ppermute | solution.py:12
  270.1 1.7 collective-permute-done
  271.8 14.5 %all_gather.18 = bf16[24,8192]{1,0:T(8,128)(2,1)S(1)} all-gather(bf16[24,1024]{1,0:T(8,128)(2,1)S(1)} %dynamic-slice_select_fusion.2), channel_id=1, replica_groups=mesh['parts'=2,'tensor'=4,'section'=2,'rows'=2] {'tensor','rows'}, dimensions={1}, use_global_device_ids=true | all-gather | bytes 442368 | tf_op jit(solution)/shard_map/while/body/eval_jaxpr/all_gather | solution.py:54
  286.7 8.1 %fusion.37 = f32[24,1024]{1,0:T(8,128)S(1)} fusion(bf16[24,8192]{1,0:T(8,128)(2,1)S(1)} %fusion.36, bf16[1,8192,1024]{2,1,0:T(8,128)(2,1)} %get-tuple-element.482, bf16[24,1024]{1,0:T(8,128)(2,1)S(1)} %dynamic-slice_select_fusion.2), kind=kOutput, calls=%fused_computation.5.clone.1 | convolution fusion | flops 402702336 | bytes 17317888 | tf_op jit(solution)/shard_map/while/body/eval_jaxpr/dot_general | solution.py:60
  295.1 26.4 %psum.22 = bf16[24,32]{1,0:T(8,128)(2,1)S(1)} all-reduce(f32[24,32]{1,0:T(8,128)S(1)} %fusion.38), channel_id=1, replica_groups=mesh['parts'=2,'tensor'=4,'section'=2,'rows'=2] {'tensor','rows'}, use_global_device_ids=true, to_apply=%region_4.4 | all-reduce | flops 768 | bytes 4608 | tf_op jit(solution)/shard_map/while/body/eval_jaxpr/psum | solution.py:68
  321.7 4.2 %collective-permute-start = (bf16[24,1024]{1,0:T(8,128)(2,1)S(1)}, bf16[24,1024]{1,0:T(8,128)(2,1)S(1)}, u32[]{:S(2)}, u32[]{:S(2)}) collective-permute-start(bf16[24,1024]{1,0:T(8,128)(2,1)S(1)} %get-tuple-element.437), channel_id=1, source_target_pairs={{0,2},{1,3},{4,6},{5,7},{8,10},{9,11},{12,14},{13,15},{16,18},{17,... | collective-permute-start | bytes 147464 | tf_op jit(solution)/shard_map/while/body/eval_jaxpr/ppermute | solution.py:12
  326.0 1.7 collective-permute-done
  328.4 20.3 %all-reduce.2.cloned.1.call-done = bf16[48,1024]{1,0:T(8,128)(2,1)} async-done(((bf16[48,1024]{1,0:T(8,128)(2,1)}), bf16[48,1024]{1,0:T(8,128)(2,1)}) %all-reduce.2.cloned.1.call-update) | async-done | bytes 98320 | tf_op jit(solution)/shard_map/psum | solution.py:17
  (49 shorter events, 6.9 us)
Async XLA Ops:
  16.2 54.4 %copy-start.2 = (bf16[1,1,32,4096]{3,2,1,0:T(8,128)(2,1)S(1)}, bf16[1,1,32,4096]{3,2,1,0:T(8,128)(2,1)}, u32[]{:S(2)}) copy-start(bf16[1,1,32,4096]{3,2,1,0:T(8,128)(2,1)} %param.12) | copy-start | bytes 786436
  64.4 63.5 %all-to-all-start.1 = ((bf16[4,2,32768]{2,1,0:T(2,128)(2,1)}), bf16[4,2,32768]{2,1,0:T(2,128)(2,1)S(1)}, u32[]{:S(2)}, u32[]{:S(2)}) async-start(bf16[4,2,32768]{2,1,0:T(2,128)(2,1)} %reshape.24), calls=%async_computation.1 | async-start | bytes 1048576 | tf_op jit(solution)/shard_map/all_to_all | solution.py:42
  79.7 53.3 %copy-start.3 = (s32[4]{0:T(128)S(1)}, s32[4]{0:T(128)}, u32[]{:S(2)}) copy-start(s32[4]{0:T(128)} %param.15) | copy-start | bytes 52
  79.7 53.3 %copy-start.4 = (s32[48]{0:T(128)S(1)}, s32[48]{0:T(128)}, u32[]{:S(2)}) copy-start(s32[48]{0:T(128)} %param.14) | copy-start | bytes 580
  127.9 19.9 %all-to-all-start = ((bf16[4,2,32768]{2,1,0:T(2,128)(2,1)}), bf16[4,2,32768]{2,1,0:T(2,128)(2,1)S(1)}, u32[]{:S(2)}, u32[]{:S(2)}) async-start(bf16[4,2,32768]{2,1,0:T(2,128)(2,1)} %reshape.22), calls=%async_computation | async-start | bytes 1048576 | tf_op jit(solution)/shard_map/all_to_all | solution.py:41
  133.0 215.7 %all-reduce.2.cloned.1.call-start = ((), (), s32[]{:S(2)}) async-start(), calls=%async_computation.2 | async-start | bytes 196608 | tf_op jit(solution)/shard_map/psum | solution.py:17
  151.1 8.8 %copy-start = (f32[1,8192]{1,0:T(1,128)S(1)}, f32[1,8192]{1,0:T(1,128)}, u32[]{:S(2)}) copy-start(f32[1,8192]{1,0:T(1,128)} %param.10) | copy-start | bytes 98308
  151.1 8.8 %copy-start.1 = (bf16[48,1024]{1,0:T(8,128)(2,1)S(1)}, bf16[48,1024]{1,0:T(8,128)(2,1)}, u32[]{:S(2)}) copy-start(bf16[48,1024]{1,0:T(8,128)(2,1)} %param.9) | copy-start | bytes 294916
  210.8 5.1 %collective-permute-start = (bf16[24,1024]{1,0:T(8,128)(2,1)S(1)}, bf16[24,1024]{1,0:T(8,128)(2,1)S(1)}, u32[]{:S(2)}, u32[]{:S(2)}) collective-permute-start(bf16[24,1024]{1,0:T(8,128)(2,1)S(1)} %get-tuple-element.437), channel_id=1, source_target_pairs={{0,2},{1,3},{4,6},{5,7},{8,10},{9,11},{12,14},{13,15},{16,18},{17,... | collective-permute-start | bytes 147464 | tf_op jit(solution)/shard_map/while/body/eval_jaxpr/ppermute | solution.py:12
  265.8 6.0 %collective-permute-start = (bf16[24,1024]{1,0:T(8,128)(2,1)S(1)}, bf16[24,1024]{1,0:T(8,128)(2,1)S(1)}, u32[]{:S(2)}, u32[]{:S(2)}) collective-permute-start(bf16[24,1024]{1,0:T(8,128)(2,1)S(1)} %get-tuple-element.437), channel_id=1, source_target_pairs={{0,2},{1,3},{4,6},{5,7},{8,10},{9,11},{12,14},{13,15},{16,18},{17,... | collective-permute-start | bytes 147464 | tf_op jit(solution)/shard_map/while/body/eval_jaxpr/ppermute | solution.py:12
  321.7 6.0 %collective-permute-start = (bf16[24,1024]{1,0:T(8,128)(2,1)S(1)}, bf16[24,1024]{1,0:T(8,128)(2,1)S(1)}, u32[]{:S(2)}, u32[]{:S(2)}) collective-permute-start(bf16[24,1024]{1,0:T(8,128)(2,1)S(1)} %get-tuple-element.437), channel_id=1, source_target_pairs={{0,2},{1,3},{4,6},{5,7},{8,10},{9,11},{12,14},{13,15},{16,18},{17,... | collective-permute-start | bytes 147464 | tf_op jit(solution)/shard_map/while/body/eval_jaxpr/ppermute | solution.py:12
Sparse Core Ops, SparseCore 0:
  328.5 20.0 all-reduce.1
where the time goes:
time: 358 us; the launch traced here: 357 us
  blocking collectives  128 us (36%)
  other arithmetic  92.3 us (26%)
  local copies, waits for them, and re-layouts  45.2 us (13%)
  waiting for transfers between devices  28.4 us (8%)
  matrix products  25.9 us (7%)
  starting transfers between devices  23.2 us (6%)
  between operations  13.5 us (4%)
    unnamed x2, other arithmetic  90.5 us
    psum x3, blocking collectives, apply_layer(): lowrank = lax.psum(partial_value, ('tensor', 'rows')).astype(jnp.bfloat16)  79.9 us
    all_gather x3, blocking collectives, apply_layer(): gathered = lax.all_gather(inputs, ('tensor', 'rows'), axis=1, tiled=True)  43.4 us
    dot_general x3, matrix products, apply_layer(): jnp.dot(normalized_input, base_weight[0], preferred_element_type=jnp.floa...  24.2 us
    psum x1, waiting for transfers between devices, spread(): return lax.psum(jnp.where(mine, x, jnp.zeros_like(x)), axis)  20.3 us
    unnamed x15, local copies, waits for them, and re-layouts  13.1 us
    ppermute x3, starting transfers between devices, passed_along(): lax.ppermute(value, axis, [(source, source + steps) for source in range(i...  11.9 us
    all_to_all x2, local copies, waits for them, and re-layouts, shards(): lax.all_to_all(halves[0], 'tensor', split_axis=3, concat_axis=1, tiled=True)  8.38 us
  transfers between devices with their start and end apart: 6, of which 5 were waited for; matrix products, arithmetic and copies ran while one was open for 19% of the time, Pallas kernels for 0%

commit v1 on v0

v1 whole, which is shorter than its diff:
```python
import functools

import jax
import jax.numpy as jnp
from jax import lax
from jax.experimental import pallas as pl
from jax.experimental.pallas import tpu as pltpu
from jax.sharding import PartitionSpec as P

MESH = pl.DeviceIdType.MESH
epsilon = 1e-05
column_tile = 256


def crossed(position, offset, count):
    result = position
    bit = 1
    while bit < count:
        if offset & bit:
            result = result + bit - 2 * bit * lax.rem(lax.div(position, bit), 2)
        bit *= 2
    return result


def kernel(
    sections,
    tensors,
    tokens_ref,
    gain_ref,
    weight_ref,
    down_ref,
    up_ref,
    row_ref,
    slot_ref,
    out_ref,
    x_buf,
    w_buf,
    gain_buf,
    down_buf,
    up_buf,
    acc,
    normed,
    score,
    score_sib,
    low_buf,
    chain_buf,
    out_buf,
    token_sem,
    gain_sem,
    down_sem,
    w_sem,
    x_send,
    x_recv,
    fwd_send,
    fwd_recv,
    up_send,
    up_recv,
    up_local,
    score_send,
    score_recv,
    low_send,
    low_recv,
    chain_send,
    chain_recv,
    out_send,
    out_recv,
    out_local,
):
    s = lax.axis_index("section")
    t = lax.axis_index("tensor")
    h = lax.axis_index("rows")
    other = 1 - h
    rows, width = x_buf.shape[2], x_buf.shape[3]
    rank = down_buf.shape[0]
    me = t * 2 + h
    peers = [crossed(t, j, tensors) for j in range(tensors)]

    def block_of(j, hh):
        return peers[j] * 2 + (h if hh == 0 else other)

    token_copy = pltpu.make_async_copy(tokens_ref, x_buf.at[0, 0], token_sem)

    @pl.when(s == 0)
    def _():
        token_copy.start()

    gain_copy = pltpu.make_async_copy(gain_ref, gain_buf, gain_sem)
    gain_copy.start()
    down_copy = pltpu.make_async_copy(down_ref.at[0, 0], down_buf, down_sem)
    down_copy.start()

    def w_copy(j, hh):
        first = pl.multiple_of(block_of(j, hh) * width, width)
        return pltpu.make_async_copy(
            weight_ref.at[0, pl.ds(first, width), :], w_buf.at[j, hh], w_sem.at[j, hh]
        )

    for j in range(tensors):
        for hh in range(2):
            w_copy(j, hh).start()

    barrier = pltpu.get_barrier_semaphore()
    for j in range(tensors):
        for hh in range(2):
            if j or hh:
                pl.semaphore_signal(
                    barrier,
                    inc=1,
                    device_id={"tensor": peers[j], "rows": h if hh == 0 else other},
                    device_id_type=MESH,
                )
    for step in range(1, sections):
        pl.semaphore_signal(
            barrier,
            inc=1,
            device_id={"section": lax.rem(s + step, sections)},
            device_id_type=MESH,
        )
    pl.semaphore_wait(barrier, 2 * tensors - 1 + sections - 1)

    def up_remote(i):
        dest = h * tensors + i
        return pltpu.make_async_remote_copy(
            src_ref=up_ref.at[0, 0, :, pl.ds(i * width, width)],
            dst_ref=up_buf.at[t],
            send_sem=up_send.at[i],
            recv_sem=up_recv.at[t],
            device_id={"tensor": lax.div(dest, 2), "rows": lax.rem(dest, 2)},
            device_id_type=MESH,
        )

    def up_here(i):
        return pltpu.make_async_copy(
            up_ref.at[0, 0, :, pl.ds(i * width, width)], up_buf.at[t], up_local
        )

    def send_up():
        for i in range(tensors):

            @pl.when(h * tensors + i != me)
            def _():
                up_remote(i).start()

            @pl.when(h * tensors + i == me)
            def _():
                up_here(i).start()

    def chain():
        return pltpu.make_async_remote_copy(
            src_ref=chain_buf,
            dst_ref=x_buf.at[0, 0],
            send_sem=chain_send,
            recv_sem=chain_recv,
            device_id={"section": lax.rem(s + 1, sections)},
            device_id_type=MESH,
        )

    def x_copy(j):
        return pltpu.make_async_remote_copy(
            src_ref=x_buf.at[0, 0],
            dst_ref=x_buf.at[j, 0],
            send_sem=x_send.at[j],
            recv_sem=x_recv.at[j],
            device_id={"tensor": peers[j]},
            device_id_type=MESH,
        )

    def fwd_copy(j):
        return pltpu.make_async_remote_copy(
            src_ref=x_buf.at[j, 0],
            dst_ref=x_buf.at[j, 1],
            send_sem=fwd_send.at[j],
            recv_sem=fwd_recv.at[j],
            device_id={"rows": other},
            device_id_type=MESH,
        )

    @pl.when(s > 0)
    def _():
        send_up()
        chain().wait_recv()

    @pl.when(s == 0)
    def _():
        token_copy.wait()

    for j in range(1, tensors):
        x_copy(j).start()
    fwd_copy(0).start()

    @pl.when(s == 0)
    def _():
        send_up()

    row = row_ref[...]
    slot_row = jnp.zeros_like(row)
    for a in range(slot_ref.shape[1]):
        slot_row = jnp.where(row == a, slot_ref[0, a], slot_row)
    grid_shape = (rows, rows)
    diagonal = lax.broadcasted_iota(jnp.int32, grid_shape, 0) == lax.broadcasted_iota(
        jnp.int32, grid_shape, 1
    )
    spread = jnp.broadcast_to(slot_row.astype(jnp.float32), grid_shape)
    slot_column = jnp.sum(jnp.where(diagonal, spread, 0.0), axis=1, keepdims=True)
    hot_here = (slot_column == t.astype(jnp.float32)).astype(jnp.float32)

    gain_copy.wait()
    down_copy.wait()
    score[...] = jnp.zeros_like(score)
    squares = jnp.zeros((rows, 1), jnp.float32)
    for j in range(tensors):
        for hh in range(2):
            if hh == 0 and j > 0:
                x_copy(j).wait_recv()
                fwd_copy(j).start()
            if hh == 1:
                fwd_copy(j).wait_recv()
            block = block_of(j, hh)
            values = x_buf[j, hh].astype(jnp.float32)
            squares = squares + jnp.sum(values * values, axis=1, keepdims=True)
            gains = gain_buf[:, pl.ds(pl.multiple_of(block * width, width), width)]
            normed[...] = (values * gains).astype(jnp.bfloat16)
            w_copy(j, hh).wait()
            first = j == 0 and hh == 0

            @pl.loop(0, width // column_tile)
            def _(n):
                columns = pl.ds(pl.multiple_of(n * column_tile, column_tile), column_tile)
                part = jnp.dot(
                    normed[...], w_buf[j, hh, :, columns], preferred_element_type=jnp.float32
                )
                acc[:, columns] = part if first else acc[:, columns] + part

            @pl.when(lax.div(block, tensors) == h)
            def _():
                place = pl.multiple_of((block - h * tensors) * width, width)
                score[...] += lax.dot_general(
                    normed[...],
                    down_buf[:, pl.ds(place, width)],
                    (((1,), (1,)), ((), ())),
                    preferred_element_type=jnp.float32,
                )

    scale = lax.rsqrt(squares / (2 * tensors * width) + epsilon)

    score_copy = pltpu.make_async_remote_copy(
        src_ref=score,
        dst_ref=score_sib,
        send_sem=score_send,
        recv_sem=score_recv,
        device_id={"rows": other},
        device_id_type=MESH,
    )
    score_copy.start()
    score_copy.wait_recv()
    low_buf[0] = (hot_here * (score[...] + score_sib[...]) * scale).astype(jnp.bfloat16)

    def low_copy(j):
        return pltpu.make_async_remote_copy(
            src_ref=low_buf.at[0],
            dst_ref=low_buf.at[j],
            send_sem=low_send.at[j],
            recv_sem=low_recv.at[j],
            device_id={"tensor": peers[j]},
            device_id_type=MESH,
        )

    for j in range(1, tensors):
        low_copy(j).start()

    half_here = lax.div(me, tensors)
    for k in range(tensors):
        local = (t == k) & (h == half_here)

        @pl.when(local)
        def _():
            up_here(0).wait()

        @pl.when(jnp.logical_not(local))
        def _():
            pltpu.make_async_remote_copy(
                src_ref=up_buf.at[k],
                dst_ref=up_buf.at[k],
                send_sem=up_send.at[0],
                recv_sem=up_recv.at[k],
                device_id={"rows": other},
                device_id_type=MESH,
            ).wait_recv()

    total = x_buf[0, 0].astype(jnp.float32) + scale * acc[...]
    for j in range(tensors):
        if j > 0:
            low_copy(j).wait_recv()
        total = total + 0.5 * jnp.dot(
            low_buf[j], up_buf[peers[j]], preferred_element_type=jnp.float32
        )

    @pl.when(s < sections - 1)
    def _():
        chain_buf[...] = total.astype(jnp.bfloat16)
        chain().start()

    share = rows // sections

    def out_copy(d):
        return pltpu.make_async_remote_copy(
            src_ref=out_buf.at[d],
            dst_ref=out_ref,
            send_sem=out_send.at[d],
            recv_sem=out_recv,
            device_id={"section": d},
            device_id_type=MESH,
        )

    @pl.when(s == sections - 1)
    def _():
        for d in range(sections):
            out_buf[d] = total[d * share : (d + 1) * share].astype(jnp.bfloat16)
        here = pltpu.make_async_copy(out_buf.at[sections - 1], out_ref, out_local)
        here.start()
        for d in range(sections - 1):
            out_copy(d).start()
        here.wait()
        for d in range(sections - 1):
            out_copy(d).wait_send()

    for j in range(tensors):
        if j > 0:
            x_copy(j).wait_send()
            low_copy(j).wait_send()
        fwd_copy(j).wait_send()
    score_copy.wait_send()
    for i in range(tensors):

        @pl.when(h * tensors + i != me)
        def _():
            up_remote(i).wait_send()

    @pl.when(s < sections - 1)
    def _():
        chain().wait_send()
        out_copy(0).wait_recv()


def solution(mesh):
    sections, tensors = mesh.shape["section"], mesh.shape["tensor"]

    def shards(tokens, gain, base_weight, down, up, row_adapter, adapter_slot):
        rows, width = tokens.shape
        features = gain.shape[1]
        rank = down.shape[2]
        bf16, f32 = jnp.bfloat16, jnp.float32
        dma = pltpu.SemaphoreType.DMA
        hbm = pl.BlockSpec(memory_space=pl.ANY)
        vmem = pl.BlockSpec(memory_space=pltpu.VMEM)
        smem = pl.BlockSpec(memory_space=pltpu.SMEM)
        return pl.pallas_call(
            functools.partial(kernel, sections, tensors),
            out_shape=jax.ShapeDtypeStruct((rows // sections, width), bf16),
            in_specs=[hbm, hbm, hbm, hbm, hbm, vmem, smem],
            out_specs=hbm,
            scratch_shapes=[
                pltpu.VMEM((tensors, 2, rows, width), bf16),
                pltpu.VMEM((tensors, 2, width, width), bf16),
                pltpu.VMEM((1, features), f32),
                pltpu.VMEM((rank, down.shape[3]), bf16),
                pltpu.VMEM((tensors, rank, width), bf16),
                pltpu.VMEM((rows, width), f32),
                pltpu.VMEM((rows, width), bf16),
                pltpu.VMEM((rows, rank), f32),
                pltpu.VMEM((rows, rank), f32),
                pltpu.VMEM((tensors, rows, rank), bf16),
                pltpu.VMEM((rows, width), bf16),
                pltpu.VMEM((sections, rows // sections, width), bf16),
                dma,
                dma,
                dma,
                dma((tensors, 2)),
                dma((tensors,)),
                dma((tensors,)),
                dma((tensors,)),
                dma((tensors,)),
                dma((tensors,)),
                dma((tensors,)),
                dma,
                dma,
                dma,
                dma((tensors,)),
                dma((tensors,)),
                dma,
                dma,
                dma((sections,)),
                dma,
                dma,
            ],
            compiler_params=pltpu.CompilerParams(
                collective_id=0, has_side_effects=True, vmem_limit_bytes=48 * 1024 * 1024
            ),
        )(
            tokens,
            gain,
            base_weight,
            down,
            up,
            row_adapter.reshape(1, rows),
            adapter_slot.reshape(1, -1),
        )

    return jax.shard_map(
        shards,
        mesh=mesh,
        in_specs=(
            P("parts", ("tensor", "rows")),
            P("section", None),
            P("section", None, ("tensor", "rows")),
            P("section", "tensor", None, "rows"),
            P("section", "tensor", None, "rows"),
            P("parts"),
            P(),
        ),
        out_specs=P(("parts", "section"), ("tensor", "rows")),
        check_vma=False,
    )
```

time: 358 us -> 56.1 us (0.16)
  blocking collectives: 128 us -> 0 us
  other arithmetic: 92.3 us -> 0 us
  Pallas kernels: 0 us -> 50.3 us
  local copies, waits for them, and re-layouts: 45.2 us -> 5.48 us
  waiting for transfers between devices: 28.4 us -> 0 us
  matrix products: 25.9 us -> 0 us
  starting transfers between devices: 23.2 us -> 0 us
  between operations: 13.5 us -> 0.02 us
    unnamed x2 -> x0, other arithmetic: 90.5 us -> none
    psum x3 -> x0, blocking collectives: 79.9 us -> none  [apply_layer(): lowrank = lax.psum(partial_value, ('tensor', 'rows')).astype(jnp.bfloat16)]
    pallas_call x0 -> x1, Pallas kernels: none -> 50.3 us  [shards(): pl.pallas_call(functools.partial(kernel, sections, tensors), out_shape=ja...]
    all_gather x5 -> x0, blocking collectives: 48.2 us -> none  [the longest x3 43.4 us: apply_layer(): gathered = lax.all_gather(inputs, ('tensor', 'rows'), axis=1, tiled=True)]
    dot_general x9 -> x0, matrix products: 25.9 us -> none  [the longest x3 24.2 us: apply_layer(): jnp.dot(normalized_input, base_weight[0], preferred_element_type=jnp.floa...]
    psum x1 -> x0, waiting for transfers between devices: 20.3 us -> none  [spread(): return lax.psum(jnp.where(mine, x, jnp.zeros_like(x)), axis)]
    all_to_all x4 -> x0, local copies, waits for them, and re-layouts: 16.7 us -> none  [the longest x2 8.38 us: shards(): lax.all_to_all(halves[0], 'tensor', split_axis=3, concat_axis=1, tiled=True)]
    all_gather x2 -> x0, local copies, waits for them, and re-layouts: 13.4 us -> none  [the longest x1 6.7 us: shards(): lax.all_gather(down_weight_slots, 'rows', axis=3, tiled=True)]
  transfers between devices with their start and end apart: 6 -> 0, of which waited for: 5 -> 0; matrix products, arithmetic and copies ran while one was open for 19% -> 0% of each run, Pallas kernels for 0% -> 0%
where the time goes in v1:
time: 56.1 us; the launch traced here: 55.8 us
  Pallas kernels  50.3 us (90%)
  local copies, waits for them, and re-layouts  5.48 us (10%)
    pallas_call x1, Pallas kernels, shards(): pl.pallas_call(functools.partial(kernel, sections, tensors), out_shape=ja...  50.3 us
    unnamed x13, local copies, waits for them, and re-layouts  5.48 us

profile of v1, /device:TPU:0, one launch (start us, length us, event | category | flops | bytes accessed | tf_op | source)
XLA Modules:
  0.0 55.8 jit_solution(2594733571209509934)
XLA Ops:
  0.0 0.0 copy-start
  0.0 0.9 %copy-done = bf16[1,1,32,4096]{3,2,1,0:T(8,128)(2,1)S(1)} copy-done((bf16[1,1,32,4096]{3,2,1,0:T(8,128)(2,1)S(1)}, bf16[1,1,32,4096]{3,2,1,0:T(8,128)(2,1)}, u32[]{:S(2)}) %copy-start) | copy-done | bytes 262168
  1.0 0.0 copy-start.1
  1.0 0.9 %copy-done.1 = bf16[1,1,32,4096]{3,2,1,0:T(8,128)(2,1)S(1)} copy-done((bf16[1,1,32,4096]{3,2,1,0:T(8,128)(2,1)S(1)}, bf16[1,1,32,4096]{3,2,1,0:T(8,128)(2,1)}, u32[]{:S(2)}) %copy-start.1) | copy-done | bytes 262168
  1.9 0.0 copy-start.2
  1.9 0.9 %copy-done.2 = bf16[48,1024]{1,0:T(8,128)(2,1)S(1)} copy-done((bf16[48,1024]{1,0:T(8,128)(2,1)S(1)}, bf16[48,1024]{1,0:T(8,128)(2,1)}, u32[]{:S(2)}) %copy-start.2) | copy-done | bytes 98328
  2.8 0.0 copy-start.3
  2.8 0.8 %copy-done.3 = f32[1,8192]{1,0:T(1,128)S(1)} copy-done((f32[1,8192]{1,0:T(1,128)S(1)}, f32[1,8192]{1,0:T(1,128)}, u32[]{:S(2)}) %copy-start.3) | copy-done | bytes 32792
  3.6 0.0 copy-start.4
  3.6 0.7 %copy-done.4 = s32[48]{0:T(128)S(1)} copy-done((s32[48]{0:T(128)S(1)}, s32[48]{0:T(128)}, u32[]{:S(2)}) %copy-start.4) | copy-done | bytes 216
  4.2 0.0 copy-start.5
  4.2 0.7 %copy-done.5 = s32[4]{0:T(128)S(1)} copy-done((s32[4]{0:T(128)S(1)}, s32[4]{0:T(128)}, u32[]{:S(2)}) %copy-start.5) | copy-done | bytes 40
  4.9 50.3 %shard_map.73 = bf16[24,1024]{1,0:T(8,128)(2,1)S(1)} custom-call(bf16[48,1024]{1,0:T(8,128)(2,1)S(1)} %copy-done.2, f32[1,8192]{1,0:T(1,128)S(1)} %copy-done.3, bf16[1,8192,1024]{2,1,0:T(8,128)(2,1)} %weight_ref.1, bf16[1,1,32,4096]{3,2,1,0:T(8,128)(2,1)S(1)} %copy-done, bf16[1,1,32,4096]{3,2,1,0:T(8,128)(2,1)S(1)} %copy-done.1, s32[1,48]{1,0:T(1,128)S(1)} %bitcast.2, ...), custom_call_target="tpu_custom_call" | custom-call | tf_op jit(solution)/shard_map/pallas_call | solution.py:357
  55.2 0.6 %copy.9 = bf16[24,1024]{1,0:T(8,128)(2,1)} copy(bf16[24,1024]{1,0:T(8,128)(2,1)S(1)} %shard_map.73) | data formatting | bytes 98304
Async XLA Ops:
  0.0 0.9 %copy-start = (bf16[1,1,32,4096]{3,2,1,0:T(8,128)(2,1)S(1)}, bf16[1,1,32,4096]{3,2,1,0:T(8,128)(2,1)}, u32[]{:S(2)}) copy-start(bf16[1,1,32,4096]{3,2,1,0:T(8,128)(2,1)} %down_ref.1) | copy-start | bytes 786436
  1.0 0.9 %copy-start.1 = (bf16[1,1,32,4096]{3,2,1,0:T(8,128)(2,1)S(1)}, bf16[1,1,32,4096]{3,2,1,0:T(8,128)(2,1)}, u32[]{:S(2)}) copy-start(bf16[1,1,32,4096]{3,2,1,0:T(8,128)(2,1)} %up_ref.1) | copy-start | bytes 786436
  1.9 0.9 %copy-start.2 = (bf16[48,1024]{1,0:T(8,128)(2,1)S(1)}, bf16[48,1024]{1,0:T(8,128)(2,1)}, u32[]{:S(2)}) copy-start(bf16[48,1024]{1,0:T(8,128)(2,1)} %tokens_ref.1) | copy-start | bytes 294916
  2.8 0.8 %copy-start.3 = (f32[1,8192]{1,0:T(1,128)S(1)}, f32[1,8192]{1,0:T(1,128)}, u32[]{:S(2)}) copy-start(f32[1,8192]{1,0:T(1,128)} %gain_ref.1) | copy-start | bytes 98308
  3.6 0.7 %copy-start.4 = (s32[48]{0:T(128)S(1)}, s32[48]{0:T(128)}, u32[]{:S(2)}) copy-start(s32[48]{0:T(128)} %param.12) | copy-start | bytes 580
  4.2 0.7 %copy-start.5 = (s32[4]{0:T(128)S(1)}, s32[4]{0:T(128)}, u32[]{:S(2)}) copy-start(s32[4]{0:T(128)} %param.13) | copy-start | bytes 52

commit v2 on v1

v2 whole, which is shorter than its diff:
```python
import functools

import jax
import jax.numpy as jnp
from jax import lax
from jax.experimental import pallas as pl
from jax.experimental.pallas import tpu as pltpu
from jax.sharding import PartitionSpec as P

MESH = pl.DeviceIdType.MESH
epsilon = 1e-05


def crossed(position, offset, count):
    result = position
    bit = 1
    while bit < count:
        if offset & bit:
            result = result + bit - 2 * bit * lax.rem(lax.div(position, bit), 2)
        bit *= 2
    return result


def kernel(
    sections,
    tensors,
    tokens_ref,
    gain_ref,
    weight_ref,
    down_ref,
    up_ref,
    row_ref,
    slot_ref,
    out_ref,
    x_buf,
    w_buf,
    gain_buf,
    down_buf,
    up_buf,
    acc,
    normed,
    low_buf,
    chain_buf,
    out_buf,
    row_buf,
    slot_buf,
    token_sem,
    row_sem,
    slot_sem,
    gain_sem,
    down_sem,
    w_sem,
    x_send,
    x_recv,
    fwd_send,
    fwd_recv,
    up_send,
    up_recv,
    up_local,
    down_send,
    down_recv,
    low_send,
    low_recv,
    chain_send,
    out_send,
    out_recv,
    out_local,
):
    s = lax.axis_index("section")
    t = lax.axis_index("tensor")
    h = lax.axis_index("rows")
    other = 1 - h
    chunks, rows, piece = x_buf.shape[0], x_buf.shape[3], x_buf.shape[4]
    width = chunks * piece
    own_chunks = chunks // 2 if sections > 1 else chunks
    me = t * 2 + h
    peers = [crossed(t, j, tensors) for j in range(tensors)]
    pairs = [(j, hh) for j in range(tensors) for hh in range(2)]
    last = sections - 1

    def block_of(j, hh):
        return peers[j] * 2 + (h if hh == 0 else other)

    def token_copy(c):
        return pltpu.make_async_copy(
            tokens_ref.at[:, pl.ds(c * piece, piece)], x_buf.at[c, 0, 0], token_sem.at[c]
        )

    @pl.when(s == 0)
    def _():
        for c in range(chunks):
            token_copy(c).start()

    row_copy = pltpu.make_async_copy(row_ref, row_buf, row_sem)
    row_copy.start()
    slot_copy = pltpu.make_async_copy(slot_ref, slot_buf, slot_sem)
    slot_copy.start()
    gain_copy = pltpu.make_async_copy(gain_ref, gain_buf, gain_sem)
    gain_copy.start()
    down_copy = pltpu.make_async_copy(down_ref.at[0, 0], down_buf.at[h], down_sem)
    down_copy.start()

    def w_copy(c, j, hh):
        first = pl.multiple_of(block_of(j, hh) * width + c * piece, piece)
        return pltpu.make_async_copy(
            weight_ref.at[0, pl.ds(first, piece), :],
            w_buf.at[c, pl.ds((2 * j + hh) * piece, piece), :],
            w_sem.at[c, 2 * j + hh],
        )

    for c in range(chunks):
        for j, hh in pairs:
            w_copy(c, j, hh).start()

    barrier = pltpu.get_barrier_semaphore()

    def greet(device):
        pl.semaphore_signal(barrier, inc=1, device_id=device, device_id_type=MESH)

    for j, hh in pairs:
        if j or hh:
            greet({"tensor": peers[j], "rows": h if hh == 0 else other})
    expected = 2 * tensors - 1
    if sections > 1:

        @pl.when(s > 0)
        def _():
            for j in range(tensors):
                greet({"section": s - 1, "tensor": peers[j]})

        @pl.when(s < last)
        def _():
            for j in range(tensors):
                greet({"section": s + 1, "tensor": peers[j]})

        expected = expected + tensors * (
            jnp.where(s > 0, 1, 0) + jnp.where(s < last, 1, 0)
        )
    if sections > 2:

        @pl.when(s == last)
        def _():
            for d in range(last - 1):
                greet({"section": d})

        @pl.when(s < last - 1)
        def _():
            greet({"section": last})

        expected = (
            expected + jnp.where(s == last, last - 1, 0) + jnp.where(s < last - 1, 1, 0)
        )
    pl.semaphore_wait(barrier, expected)

    def token_send(c, j):
        return pltpu.make_async_remote_copy(
            src_ref=tokens_ref.at[:, pl.ds(c * piece, piece)],
            dst_ref=x_buf.at[c, j, 0],
            send_sem=x_send.at[c, j],
            recv_sem=x_recv.at[c, j],
            device_id={"section": 0, "tensor": peers[j]},
            device_id_type=MESH,
        )

    def chain(c, j):
        return pltpu.make_async_remote_copy(
            src_ref=chain_buf.at[c],
            dst_ref=x_buf.at[c, j, 0],
            send_sem=chain_send.at[c, j],
            recv_sem=x_recv.at[c, j],
            device_id={"section": lax.rem(s + 1, sections), "tensor": peers[j]},
            device_id_type=MESH,
        )

    def fwd_copy(c, j):
        return pltpu.make_async_remote_copy(
            src_ref=x_buf.at[c, j, 0],
            dst_ref=x_buf.at[c, j, 1],
            send_sem=fwd_send.at[c, j],
            recv_sem=fwd_recv.at[c, j],
            device_id={"rows": other},
            device_id_type=MESH,
        )

    @pl.when(s == 0)
    def _():
        for c in range(own_chunks):
            for j in range(1, tensors):
                token_send(c, j).start()

    if sections > 1:

        @pl.when(s == 1)
        def _():
            for c in range(own_chunks, chunks):
                for j in range(1, tensors):
                    token_send(c, j).start()

    down_remote = pltpu.make_async_remote_copy(
        src_ref=down_ref.at[0, 0],
        dst_ref=down_buf.at[h],
        send_sem=down_send,
        recv_sem=down_recv,
        device_id={"rows": other},
        device_id_type=MESH,
    )
    down_remote.start()

    def up_remote(i):
        dest = h * tensors + i
        return pltpu.make_async_remote_copy(
            src_ref=up_ref.at[0, 0, :, pl.ds(i * width, width)],
            dst_ref=up_buf.at[t],
            send_sem=up_send.at[i],
            recv_sem=up_recv.at[t],
            device_id={"tensor": lax.div(dest, 2), "rows": lax.rem(dest, 2)},
            device_id_type=MESH,
        )

    def up_here(i):
        return pltpu.make_async_copy(
            up_ref.at[0, 0, :, pl.ds(i * width, width)], up_buf.at[t], up_local
        )

    for i in range(tensors):

        @pl.when(h * tensors + i != me)
        def _():
            up_remote(i).start()

        @pl.when(h * tensors + i == me)
        def _():
            up_here(i).start()

    row_copy.wait()
    slot_copy.wait()
    row = row_buf[...]
    slots = slot_buf[...]
    slot_row = jnp.zeros_like(row)
    for a in range(slots.shape[1]):
        slot_row = jnp.where(row == a, slots[:, a : a + 1], slot_row)
    grid_shape = (rows, rows)
    diagonal = lax.broadcasted_iota(jnp.int32, grid_shape, 0) == lax.broadcasted_iota(
        jnp.int32, grid_shape, 1
    )
    spread = jnp.broadcast_to(slot_row.astype(jnp.float32), grid_shape)
    slot_column = jnp.sum(jnp.where(diagonal, spread, 0.0), axis=1, keepdims=True)
    hot_here = (slot_column == t.astype(jnp.float32)).astype(jnp.float32)

    gain_copy.wait()
    down_copy.wait()
    down_remote.wait_recv()
    squares = jnp.zeros((rows, piece), jnp.float32)
    score = jnp.zeros((rows, down_buf.shape[1]), jnp.float32)

    def low_copy(j):
        return pltpu.make_async_remote_copy(
            src_ref=low_buf.at[0],
            dst_ref=low_buf.at[j],
            send_sem=low_send.at[j],
            recv_sem=low_recv.at[j],
            device_id={"tensor": peers[j]},
            device_id_type=MESH,
        )

    for c in range(chunks):

        @pl.when(s == 0)
        def _():
            token_copy(c).wait()

        @pl.when(s > 0)
        def _():
            x_recv_own = chain(c, 0)
            x_recv_own.wait_recv()

        fwd_copy(c, 0).start()
        for j in range(1, tensors):
            chain(c, j).wait_recv()
            fwd_copy(c, j).start()
        for hh in range(2):
            for j in range(tensors):
                if hh == 1:
                    fwd_copy(c, j).wait_recv()
                values = x_buf[c, j, hh].astype(jnp.float32)
                squares = squares + values * values
                place = pl.multiple_of(block_of(j, hh) * width + c * piece, piece)
                normed[:, (2 * j + hh) * piece : (2 * j + hh + 1) * piece] = (
                    values * gain_buf[:, pl.ds(place, piece)]
                ).astype(jnp.bfloat16)
        downs = []
        for j, hh in pairs:
            block = block_of(j, hh)
            place = pl.multiple_of(lax.rem(block, tensors) * width + c * piece, piece)
            downs.append(down_buf[lax.div(block, tensors), :, pl.ds(place, piece)])
        score = score + lax.dot_general(
            normed[...],
            jnp.concatenate(downs, axis=1),
            (((1,), (1,)), ((), ())),
            preferred_element_type=jnp.float32,
        )
        if c == chunks - 1:
            mean_square = jnp.sum(squares, axis=1, keepdims=True) / (2 * tensors * width)
            scale = lax.rsqrt(mean_square + epsilon)
            low_buf[0] = (hot_here * score * scale).astype(jnp.bfloat16)
            for j in range(1, tensors):
                low_copy(j).start()
        for j, hh in pairs:
            w_copy(c, j, hh).wait()
        part = jnp.dot(normed[...], w_buf[c], preferred_element_type=jnp.float32)
        acc[...] = part if c == 0 else acc[...] + part

    half_here = lax.div(me, tensors)
    for k in range(tensors):
        local = (t == k) & (h == half_here)

        @pl.when(local)
        def _():
            up_here(0).wait()

        @pl.when(jnp.logical_not(local))
        def _():
            pltpu.make_async_remote_copy(
                src_ref=up_buf.at[k],
                dst_ref=up_buf.at[k],
                send_sem=up_send.at[0],
                recv_sem=up_recv.at[k],
                device_id={"rows": other},
                device_id_type=MESH,
            ).wait_recv()

    for j in range(1, tensors):
        low_copy(j).wait_recv()

    share = rows // sections
    for c in range(chunks):
        columns = slice(c * piece, (c + 1) * piece)
        update = jnp.zeros((rows, piece), jnp.float32)
        for j in range(tensors):
            update = update + jnp.dot(
                low_buf[j], up_buf[peers[j], :, columns], preferred_element_type=jnp.float32
            )
        total = x_buf[c, 0, 0].astype(jnp.float32) + scale * acc[:, columns] + 0.5 * update

        @pl.when(s < last)
        def _():
            chain_buf[c] = total.astype(jnp.bfloat16)
            for j in range(tensors):
                chain(c, j).start()

        @pl.when(s == last)
        def _():
            for d in range(sections):
                out_buf[d, :, columns] = total[d * share : (d + 1) * share].astype(jnp.bfloat16)

    def out_copy(d):
        return pltpu.make_async_remote_copy(
            src_ref=out_buf.at[d],
            dst_ref=out_ref,
            send_sem=out_send.at[d],
            recv_sem=out_recv,
            device_id={"section": d},
            device_id_type=MESH,
        )

    @pl.when(s == last)
    def _():
        for d in range(last):
            out_copy(d).start()
        here = pltpu.make_async_copy(out_buf.at[last], out_ref, out_local)
        here.start()
        here.wait()
        for d in range(last):
            out_copy(d).wait_send()

    @pl.when(s == 0)
    def _():
        for c in range(own_chunks):
            for j in range(1, tensors):
                token_send(c, j).wait_send()

    if sections > 1:

        @pl.when(s == 1)
        def _():
            for c in range(own_chunks, chunks):
                for j in range(1, tensors):
                    token_send(c, j).wait_send()

    for c in range(chunks):
        for j in range(tensors):
            fwd_copy(c, j).wait_send()
    for j in range(1, tensors):
        low_copy(j).wait_send()
    down_remote.wait_send()
    for i in range(tensors):

        @pl.when(h * tensors + i != me)
        def _():
            up_remote(i).wait_send()

    @pl.when(s < last)
    def _():
        for c in range(chunks):
            for j in range(tensors):
                chain(c, j).wait_send()
        out_copy(0).wait_recv()


def solution(mesh):
    sections, tensors = mesh.shape["section"], mesh.shape["tensor"]

    def shards(tokens, gain, base_weight, down, up, row_adapter, adapter_slot):
        rows, width = tokens.shape
        features = gain.shape[1]
        rank = down.shape[2]
        piece = max(128, width // 4)
        chunks = width // piece
        bf16, f32 = jnp.bfloat16, jnp.float32
        dma = pltpu.SemaphoreType.DMA
        hbm = pl.BlockSpec(memory_space=pltpu.HBM)
        return pl.pallas_call(
            functools.partial(kernel, sections, tensors),
            out_shape=jax.ShapeDtypeStruct((rows // sections, width), bf16),
            in_specs=[hbm] * 7,
            out_specs=hbm,
            scratch_shapes=[
                pltpu.VMEM((chunks, tensors, 2, rows, piece), bf16),
                pltpu.VMEM((chunks, 2 * tensors * piece, width), bf16),
                pltpu.VMEM((1, features), f32),
                pltpu.VMEM((2, rank, down.shape[3]), bf16),
                pltpu.VMEM((tensors, rank, width), bf16),
                pltpu.VMEM((rows, width), f32),
                pltpu.VMEM((rows, 2 * tensors * piece), bf16),
                pltpu.VMEM((tensors, rows, rank), bf16),
                pltpu.VMEM((chunks, rows, piece), bf16),
                pltpu.VMEM((sections, rows // sections, width), bf16),
                pltpu.VMEM((1, rows), jnp.int32),
                pltpu.VMEM((1, adapter_slot.shape[0]), jnp.int32),
                dma((chunks,)),
                dma,
                dma,
                dma,
                dma,
                dma((chunks, 2 * tensors)),
                dma((chunks, tensors)),
                dma((chunks, tensors)),
                dma((chunks, tensors)),
                dma((chunks, tensors)),
                dma((tensors,)),
                dma((tensors,)),
                dma,
                dma,
                dma,
                dma((tensors,)),
                dma((tensors,)),
                dma((chunks, tensors)),
                dma((sections,)),
                dma,
                dma,
            ],
            compiler_params=pltpu.CompilerParams(
                collective_id=0, has_side_effects=True, vmem_limit_bytes=64 * 1024 * 1024
            ),
        )(
            tokens,
            gain,
            base_weight,
            down,
            up,
            row_adapter.reshape(1, rows),
            adapter_slot.reshape(1, -1),
        )

    return jax.shard_map(
        shards,
        mesh=mesh,
        in_specs=(
            P("parts", ("tensor", "rows")),
            P("section", None),
            P("section", None, ("tensor", "rows")),
            P("section", "tensor", None, "rows"),
            P("section", "tensor", None, "rows"),
            P("parts"),
            P(),
        ),
        out_specs=P(("parts", "section"), ("tensor", "rows")),
        check_vma=False,
    )
```

time: 56.1 us -> 47.3 us (0.84)
  Pallas kernels: 50.3 us -> 45.7 us
  local copies, waits for them, and re-layouts: 5.48 us -> 1.42 us
    pallas_call x1, Pallas kernels: 50.3 us -> 45.7 us  [shards(): pl.pallas_call(functools.partial(kernel, sections, tensors), out_shape=ja...]
    unnamed x13 -> x1, local copies, waits for them, and re-layouts: 5.48 us -> 1.42 us
where the time goes in v2:
time: 47.3 us; the launch traced here: 47.1 us
  Pallas kernels  45.7 us (97%)
  local copies, waits for them, and re-layouts  1.42 us (3%)
    pallas_call x1, Pallas kernels, shards(): pl.pallas_call(functools.partial(kernel, sections, tensors), out_shape=ja...  45.7 us
    unnamed x1, local copies, waits for them, and re-layouts  1.42 us

profile of v2, /device:TPU:0, one launch (start us, length us, event | category | flops | bytes accessed | tf_op | source)
XLA Modules:
  0.0 47.1 jit_solution(17741000672459088850)
XLA Ops:
  0.0 45.7 %shard_map.73 = bf16[24,1024]{1,0:T(8,128)(2,1)} custom-call(bf16[48,1024]{1,0:T(8,128)(2,1)} %tokens_ref.1, f32[1,8192]{1,0:T(1,128)} %gain_ref.1, bf16[1,8192,1024]{2,1,0:T(8,128)(2,1)} %weight_ref.1, bf16[1,1,32,4096]{3,2,1,0:T(8,128)(2,1)} %down_ref.1, bf16[1,1,32,4096]{3,2,1,0:T(8,128)(2,1)} %up_ref.1, s32[1,48]{1,0:T(1,128)} %bitcast.2, s32[1,4]{1,0:T(1,128)} %bitcast.3), custom_call_target="tpu_custom_call" | custom-call | tf_op jit(solution)/shard_map/pallas_call | solution.py:422
  45.7 1.4 %copy.9 = bf16[24,1024]{1,0:T(8,128)(2,1)} copy(bf16[24,1024]{1,0:T(8,128)(2,1)} %shard_map.73) | data formatting | bytes 98304

commit v3 on v2

v3 whole, which is shorter than its diff:
```python
import functools

import jax
import jax.numpy as jnp
from jax import lax
from jax.experimental import pallas as pl
from jax.experimental.pallas import tpu as pltpu
from jax.sharding import PartitionSpec as P

MESH = pl.DeviceIdType.MESH
epsilon = 1e-05


def crossed(position, offset, count):
    result = position
    bit = 1
    while bit < count:
        if offset & bit:
            result = result + bit - 2 * bit * lax.rem(lax.div(position, bit), 2)
        bit *= 2
    return result


def kernel(
    sections,
    tensors,
    tokens_ref,
    gain_ref,
    weight_ref,
    down_ref,
    up_ref,
    row_ref,
    slot_ref,
    out_ref,
    x_buf,
    w_buf,
    gain_buf,
    down_buf,
    up_buf,
    acc,
    normed,
    squares,
    score,
    low_buf,
    low_all,
    part_down,
    part_score,
    chain_buf,
    out_buf,
    row_buf,
    slot_buf,
    token_sem,
    row_sem,
    slot_sem,
    gain_sem,
    down_sem,
    w_sem,
    x_send,
    x_recv,
    fwd_send,
    fwd_recv,
    up_send,
    up_recv,
    up_local,
    part_down_send,
    part_down_recv,
    part_down_local,
    part_send,
    part_recv,
    down_send,
    down_recv,
    low_send,
    low_recv,
    chain_send,
    out_send,
    out_recv,
    out_local,
):
    s = lax.axis_index("section")
    t = lax.axis_index("tensor")
    h = lax.axis_index("rows")
    other = 1 - h
    chunks, rows, piece = x_buf.shape[0], x_buf.shape[3], x_buf.shape[4]
    width = chunks * piece
    own_chunks = chunks // 2 if sections > 1 else chunks
    me = t * 2 + h
    peers = [crossed(t, j, tensors) for j in range(tensors)]
    pairs = [(j, hh) for j in range(tensors) for hh in range(2)]
    last = sections - 1
    order = sorted(range(chunks), key=lambda c: (c % max(1, chunks // 2), c))

    def block_of(j, hh):
        return peers[j] * 2 + (h if hh == 0 else other)

    barrier = pltpu.get_barrier_semaphore()

    def greet(device):
        pl.semaphore_signal(barrier, inc=1, device_id=device, device_id_type=MESH)

    for j, hh in pairs:
        if j or hh:
            greet({"tensor": peers[j], "rows": h if hh == 0 else other})
    expected = 2 * tensors - 1
    if sections > 1:

        @pl.when(s > 0)
        def _():
            for j in range(tensors):
                greet({"section": s - 1, "tensor": peers[j]})

        @pl.when(s < last)
        def _():
            for j in range(tensors):
                greet({"section": s + 1, "tensor": peers[j]})

        expected = expected + tensors * (
            jnp.where(s > 0, 1, 0) + jnp.where(s < last, 1, 0)
        )
    if sections > 2:

        @pl.when(s == last)
        def _():
            for d in range(last - 1):
                greet({"section": d})

        @pl.when(s < last - 1)
        def _():
            greet({"section": last})

        expected = (
            expected + jnp.where(s == last, last - 1, 0) + jnp.where(s < last - 1, 1, 0)
        )
    def token_copy(c):
        return pltpu.make_async_copy(
            tokens_ref.at[:, pl.ds(c * piece, piece)], x_buf.at[c, 0, 0], token_sem.at[c]
        )

    @pl.when(s == 0)
    def _():
        for c in range(chunks):
            token_copy(c).start()

    row_copy = pltpu.make_async_copy(row_ref, row_buf, row_sem)
    row_copy.start()
    slot_copy = pltpu.make_async_copy(slot_ref, slot_buf, slot_sem)
    slot_copy.start()
    gain_copy = pltpu.make_async_copy(gain_ref, gain_buf, gain_sem)
    gain_copy.start()
    down_copy = pltpu.make_async_copy(down_ref.at[0, 0], down_buf.at[h], down_sem)

    @pl.when(s == 0)
    def _():
        down_copy.start()

    def w_copy(c, j, hh):
        first = pl.multiple_of(block_of(j, hh) * width + c * piece, piece)
        return pltpu.make_async_copy(
            weight_ref.at[0, pl.ds(first, piece), :],
            w_buf.at[c, pl.ds((2 * j + hh) * piece, piece), :],
            w_sem.at[c, 2 * j + hh],
        )

    for c in range(chunks):
        for j, hh in pairs:
            w_copy(c, j, hh).start()

    pl.semaphore_wait(barrier, expected)

    def token_send(c, j):
        return pltpu.make_async_remote_copy(
            src_ref=tokens_ref.at[:, pl.ds(c * piece, piece)],
            dst_ref=x_buf.at[c, j, 0],
            send_sem=x_send.at[c, j],
            recv_sem=x_recv.at[c, j],
            device_id={"section": 0, "tensor": peers[j]},
            device_id_type=MESH,
        )

    def chain(c, j):
        return pltpu.make_async_remote_copy(
            src_ref=chain_buf.at[c],
            dst_ref=x_buf.at[c, j, 0],
            send_sem=chain_send.at[c, j],
            recv_sem=x_recv.at[c, j],
            device_id={"section": lax.rem(s + 1, sections), "tensor": peers[j]},
            device_id_type=MESH,
        )

    def fwd_copy(c, j):
        return pltpu.make_async_remote_copy(
            src_ref=x_buf.at[c, j, 0],
            dst_ref=x_buf.at[c, j, 1],
            send_sem=fwd_send.at[c, j],
            recv_sem=fwd_recv.at[c, j],
            device_id={"rows": other},
            device_id_type=MESH,
        )

    @pl.when(s == 0)
    def _():
        for c in range(own_chunks):
            for j in range(1, tensors):
                token_send(c, j).start()

    if sections > 1:

        @pl.when(s == 1)
        def _():
            for c in range(own_chunks, chunks):
                for j in range(1, tensors):
                    token_send(c, j).start()

    down_remote = pltpu.make_async_remote_copy(
        src_ref=down_ref.at[0, 0],
        dst_ref=down_buf.at[h],
        send_sem=down_send,
        recv_sem=down_recv,
        device_id={"rows": other},
        device_id_type=MESH,
    )

    @pl.when(s == 0)
    def _():
        down_remote.start()

    def map_remote(i, source, landing, sent, landed):
        dest = h * tensors + i
        return pltpu.make_async_remote_copy(
            src_ref=source.at[0, 0, :, pl.ds(i * width, width)],
            dst_ref=landing.at[t],
            send_sem=sent.at[i],
            recv_sem=landed.at[t],
            device_id={"tensor": lax.div(dest, 2), "rows": lax.rem(dest, 2)},
            device_id_type=MESH,
        )

    def map_here(i, source, landing, done):
        return pltpu.make_async_copy(
            source.at[0, 0, :, pl.ds(i * width, width)], landing.at[t], done
        )

    def send_maps(source, landing, sent, landed, done):
        for i in range(tensors):

            @pl.when(h * tensors + i != me)
            def _():
                map_remote(i, source, landing, sent, landed).start()

            @pl.when(h * tensors + i == me)
            def _():
                map_here(i, source, landing, done).start()

    def wait_maps(source, landing, sent, landed, done):
        half_here = lax.div(me, tensors)
        for k in range(tensors):
            local = (t == k) & (h == half_here)

            @pl.when(local)
            def _():
                map_here(0, source, landing, done).wait()

            @pl.when(jnp.logical_not(local))
            def _():
                pltpu.make_async_remote_copy(
                    src_ref=landing.at[k],
                    dst_ref=landing.at[k],
                    send_sem=sent.at[0],
                    recv_sem=landed.at[k],
                    device_id={"rows": other},
                    device_id_type=MESH,
                ).wait_recv()

    def wait_maps_sent(source, landing, sent, landed, done):
        for i in range(tensors):

            @pl.when(h * tensors + i != me)
            def _():
                map_remote(i, source, landing, sent, landed).wait_send()

    ups = (up_ref, up_buf, up_send, up_recv, up_local)
    downs = (down_ref, part_down, part_down_send, part_down_recv, part_down_local)

    @pl.when(s > 0)
    def _():
        send_maps(*downs)

    send_maps(*ups)

    row_copy.wait()
    slot_copy.wait()
    row = row_buf[...]
    slots = slot_buf[...]
    slot_row = jnp.zeros_like(row)
    for a in range(slots.shape[1]):
        slot_row = jnp.where(row == a, slots[:, a : a + 1], slot_row)
    grid_shape = (rows, rows)
    diagonal = lax.broadcasted_iota(jnp.int32, grid_shape, 0) == lax.broadcasted_iota(
        jnp.int32, grid_shape, 1
    )
    spread = jnp.broadcast_to(slot_row.astype(jnp.float32), grid_shape)
    slot_column = jnp.sum(jnp.where(diagonal, spread, 0.0), axis=1, keepdims=True)
    hot_here = (slot_column == t.astype(jnp.float32)).astype(jnp.float32)
    rank = down_buf.shape[1]

    gain_copy.wait()

    def low_copy(j):
        return pltpu.make_async_remote_copy(
            src_ref=low_buf.at[0],
            dst_ref=low_buf.at[j],
            send_sem=low_send.at[j],
            recv_sem=low_recv.at[j],
            device_id={"tensor": peers[j]},
            device_id_type=MESH,
        )

    def part_copy(j, hh):
        return pltpu.make_async_remote_copy(
            src_ref=part_score.at[0],
            dst_ref=part_score.at[2 * j + hh],
            send_sem=part_send.at[2 * j + hh],
            recv_sem=part_recv.at[2 * j + hh],
            device_id={"tensor": peers[j], "rows": h if hh == 0 else other},
            device_id_type=MESH,
        )

    def absorb(c, j, hh):
        values = x_buf[c, j, hh].astype(jnp.float32)
        if c == 0 and j == 0 and hh == 0:
            squares[...] = values * values
        else:
            squares[...] += values * values
        place = pl.multiple_of(block_of(j, hh) * width + c * piece, piece)
        normed[c, :, (2 * j + hh) * piece : (2 * j + hh + 1) * piece] = (
            values * gain_buf[:, pl.ds(place, piece)]
        ).astype(jnp.bfloat16)

    def multiply(c):
        for j, hh in pairs:
            w_copy(c, j, hh).wait()
        part = jnp.dot(normed[c], w_buf[c], preferred_element_type=jnp.float32)
        acc[...] = part if c == order[0] else acc[...] + part

    for c in range(chunks):

        @pl.when(s == 0)
        def _():
            token_copy(c).wait()

        @pl.when(s > 0)
        def _():
            chain(c, 0).wait_recv()

        fwd_copy(c, 0).start()
        absorb(c, 0, 0)

    @pl.when(s > 0)
    def _():
        wait_maps(*downs)
        shape = (rows, tensors * rank)
        own = jnp.zeros(shape, jnp.float32)
        for c in range(chunks):
            own = own + lax.dot_general(
                normed[c, :, :piece],
                jnp.concatenate(
                    [part_down[k, :, c * piece : (c + 1) * piece] for k in range(tensors)], axis=0
                ),
                (((1,), (1,)), ((), ())),
                preferred_element_type=jnp.float32,
            )
        slot_of_lane = lax.div(lax.broadcasted_iota(jnp.int32, shape, 1), rank)
        kept = slot_of_lane.astype(jnp.float32) == slot_column
        part_score[0] = jnp.where(kept, own, 0.0).astype(jnp.bfloat16)
        for j, hh in pairs:
            if j or hh:
                part_copy(j, hh).start()

    @pl.when(s == 0)
    def _():
        down_copy.wait()
        down_remote.wait_recv()

    for step in range(chunks + 1):
        if step < chunks:
            for j in range(1, tensors):
                chain(order[step], j).wait_recv()
                fwd_copy(order[step], j).start()
        if step == 0:
            continue
        c = order[step - 1]
        for j in range(1, tensors):
            absorb(c, j, 0)
        for j in range(tensors):
            fwd_copy(c, j).wait_recv()
            absorb(c, j, 1)

        @pl.when(s == 0)
        def _():
            down_pieces = []
            for j, hh in pairs:
                block = block_of(j, hh)
                place = pl.multiple_of(lax.rem(block, tensors) * width + c * piece, piece)
                down_pieces.append(down_buf[lax.div(block, tensors), :, pl.ds(place, piece)])
            score_part = lax.dot_general(
                normed[c],
                jnp.concatenate(down_pieces, axis=1),
                (((1,), (1,)), ((), ())),
                preferred_element_type=jnp.float32,
            )
            score[...] = score_part if step == 1 else score[...] + score_part

        if step <= chunks - 2:
            multiply(c)

    mean_square = jnp.sum(squares[...], axis=1, keepdims=True) / (2 * tensors * width)
    scale = lax.rsqrt(mean_square + epsilon)

    @pl.when(s == 0)
    def _():
        low_buf[0] = (hot_here * score[...] * scale).astype(jnp.bfloat16)
        for j in range(1, tensors):
            low_copy(j).start()

    for c in order[max(chunks - 2, 0) :]:
        multiply(c)

    wait_maps(*ups)

    @pl.when(s == 0)
    def _():
        for j in range(1, tensors):
            low_copy(j).wait_recv()
        for k in range(tensors):
            low_all[:, k * rank : (k + 1) * rank] = low_buf[peers[k]]

    @pl.when(s > 0)
    def _():
        summed = part_score[0].astype(jnp.float32)
        for j, hh in pairs:
            if j or hh:
                part_copy(j, hh).wait_recv()
                summed = summed + part_score[2 * j + hh].astype(jnp.float32)
        low_all[...] = (summed * scale).astype(jnp.bfloat16)

    share = rows // sections

    def out_copy(c, d):
        return pltpu.make_async_remote_copy(
            src_ref=out_buf.at[c, d],
            dst_ref=out_ref.at[:, pl.ds(c * piece, piece)],
            send_sem=out_send.at[c, d],
            recv_sem=out_recv.at[c],
            device_id={"section": d},
            device_id_type=MESH,
        )

    def out_here(c):
        return pltpu.make_async_copy(
            out_buf.at[c, last], out_ref.at[:, pl.ds(c * piece, piece)], out_local.at[c]
        )

    for c in range(chunks):
        columns = slice(c * piece, (c + 1) * piece)
        update = jnp.dot(
            low_all[...],
            jnp.concatenate([up_buf[k, :, columns] for k in range(tensors)], axis=0),
            preferred_element_type=jnp.float32,
        )
        total = x_buf[c, 0, 0].astype(jnp.float32) + scale * acc[:, columns] + 0.5 * update

        @pl.when(s < last)
        def _():
            chain_buf[c] = total.astype(jnp.bfloat16)
            chain(c, 0).start()

        @pl.when(s == last)
        def _():
            for d in range(sections):
                out_buf[c, d] = total[d * share : (d + 1) * share].astype(jnp.bfloat16)
                if d < last:
                    out_copy(c, d).start()
                else:
                    out_here(c).start()

    @pl.when(s < last)
    def _():
        for c in order:
            for j in range(1, tensors):
                chain(c, j).start()

    @pl.when(s == last)
    def _():
        for c in range(chunks):
            out_here(c).wait()
            for d in range(last):
                out_copy(c, d).wait_send()

    @pl.when(s == 0)
    def _():
        for c in range(own_chunks):
            for j in range(1, tensors):
                token_send(c, j).wait_send()

    if sections > 1:

        @pl.when(s == 1)
        def _():
            for c in range(own_chunks, chunks):
                for j in range(1, tensors):
                    token_send(c, j).wait_send()

    for c in range(chunks):
        for j in range(tensors):
            fwd_copy(c, j).wait_send()
    wait_maps_sent(*ups)

    @pl.when(s == 0)
    def _():
        for j in range(1, tensors):
            low_copy(j).wait_send()
        down_remote.wait_send()

    @pl.when(s > 0)
    def _():
        wait_maps_sent(*downs)
        for j, hh in pairs:
            if j or hh:
                part_copy(j, hh).wait_send()

    @pl.when(s < last)
    def _():
        for c in range(chunks):
            for j in range(tensors):
                chain(c, j).wait_send()
        for c in range(chunks):
            out_copy(c, 0).wait_recv()


def solution(mesh):
    sections, tensors = mesh.shape["section"], mesh.shape["tensor"]

    def shards(tokens, gain, base_weight, down, up, row_adapter, adapter_slot):
        rows, width = tokens.shape
        features = gain.shape[1]
        rank = down.shape[2]
        piece = max(128, width // 4)
        chunks = width // piece
        bf16, f32 = jnp.bfloat16, jnp.float32
        dma = pltpu.SemaphoreType.DMA
        hbm = pl.BlockSpec(memory_space=pltpu.HBM)
        return pl.pallas_call(
            functools.partial(kernel, sections, tensors),
            out_shape=jax.ShapeDtypeStruct((rows // sections, width), bf16),
            in_specs=[hbm] * 7,
            out_specs=hbm,
            scratch_shapes=[
                pltpu.VMEM((chunks, tensors, 2, rows, piece), bf16),
                pltpu.VMEM((chunks, 2 * tensors * piece, width), bf16),
                pltpu.VMEM((1, features), f32),
                pltpu.VMEM((2, rank, down.shape[3]), bf16),
                pltpu.VMEM((tensors, rank, width), bf16),
                pltpu.VMEM((rows, width), f32),
                pltpu.VMEM((chunks, rows, 2 * tensors * piece), bf16),
                pltpu.VMEM((rows, piece), f32),
                pltpu.VMEM((rows, rank), f32),
                pltpu.VMEM((tensors, rows, rank), bf16),
                pltpu.VMEM((rows, tensors * rank), bf16),
                pltpu.VMEM((tensors, rank, width), bf16),
                pltpu.VMEM((2 * tensors, rows, tensors * rank), bf16),
                pltpu.VMEM((chunks, rows, piece), bf16),
                pltpu.VMEM((chunks, sections, rows // sections, piece), bf16),
                pltpu.VMEM((1, rows), jnp.int32),
                pltpu.VMEM((1, adapter_slot.shape[0]), jnp.int32),
                dma((chunks,)),
                dma,
                dma,
                dma,
                dma,
                dma((chunks, 2 * tensors)),
                dma((chunks, tensors)),
                dma((chunks, tensors)),
                dma((chunks, tensors)),
                dma((chunks, tensors)),
                dma((tensors,)),
                dma((tensors,)),
                dma,
                dma((tensors,)),
                dma((tensors,)),
                dma,
                dma((2 * tensors,)),
                dma((2 * tensors,)),
                dma,
                dma,
                dma((tensors,)),
                dma((tensors,)),
                dma((chunks, tensors)),
                dma((chunks, sections)),
                dma((chunks,)),
                dma((chunks,)),
            ],
            compiler_params=pltpu.CompilerParams(
                collective_id=0, has_side_effects=True, vmem_limit_bytes=64 * 1024 * 1024
            ),
        )(
            tokens,
            gain,
            base_weight,
            down,
            up,
            row_adapter.reshape(1, rows),
            adapter_slot.reshape(1, -1),
        )

    return jax.shard_map(
        shards,
        mesh=mesh,
        in_specs=(
            P("parts", ("tensor", "rows")),
            P("section", None),
            P("section", None, ("tensor", "rows")),
            P("section", "tensor", None, "rows"),
            P("section", "tensor", None, "rows"),
            P("parts"),
            P(),
        ),
        out_specs=P(("parts", "section"), ("tensor", "rows")),
        check_vma=False,
    )
```

time: 47.3 us -> 43.1 us (0.911)
  Pallas kernels: 45.7 us -> 41.6 us
    pallas_call x1, Pallas kernels: 45.7 us -> 41.6 us  [shards(): pl.pallas_call(functools.partial(kernel, sections, tensors), out_shape=ja...]
where the time goes in v3:
time: 43.1 us; the launch traced here: 43 us
  Pallas kernels  41.6 us (97%)
  local copies, waits for them, and re-layouts  1.42 us (3%)
    pallas_call x1, Pallas kernels, shards(): pl.pallas_call(functools.partial(kernel, sections, tensors), out_shape=ja...  41.6 us
    unnamed x1, local copies, waits for them, and re-layouts  1.42 us

profile of v3, /device:TPU:0, one launch (start us, length us, event | category | flops | bytes accessed | tf_op | source)
XLA Modules:
  0.0 43.0 jit_solution(14693680125759193527)
XLA Ops:
  0.0 41.6 %shard_map.73 = bf16[24,1024]{1,0:T(8,128)(2,1)} custom-call(bf16[48,1024]{1,0:T(8,128)(2,1)} %tokens_ref.1, f32[1,8192]{1,0:T(1,128)} %gain_ref.1, bf16[1,8192,1024]{2,1,0:T(8,128)(2,1)} %weight_ref.1, bf16[1,1,32,4096]{3,2,1,0:T(8,128)(2,1)} %down_ref.1, bf16[1,1,32,4096]{3,2,1,0:T(8,128)(2,1)} %up_ref.1, s32[1,48]{1,0:T(1,128)} %bitcast.2, s32[1,4]{1,0:T(1,128)} %bitcast.3), custom_call_target="tpu_custom_call" | custom-call | tf_op jit(solution)/shard_map/pallas_call | solution.py:551
  41.6 1.4 %copy.9 = bf16[24,1024]{1,0:T(8,128)(2,1)} copy(bf16[24,1024]{1,0:T(8,128)(2,1)} %shard_map.73) | data formatting | bytes 98304

commit v4 on v3

--- a/solution.py
+++ b/solution.py
@@ -87,7 +87,7 @@
     peers = [crossed(t, j, tensors) for j in range(tensors)]
     pairs = [(j, hh) for j in range(tensors) for hh in range(2)]
     last = sections - 1
-    order = sorted(range(chunks), key=lambda c: (c % max(1, chunks // 2), c))
+    order = sorted(range(chunks), key=lambda c: (c % max(1, chunks // 2), -c))
 
     def block_of(j, hh):
         return peers[j] * 2 + (h if hh == 0 else other)
@@ -183,6 +183,16 @@
             send_sem=chain_send.at[c, j],
             recv_sem=x_recv.at[c, j],
             device_id={"section": lax.rem(s + 1, sections), "tensor": peers[j]},
+            device_id_type=MESH,
+        )
+
+    def spread_copy(j):
+        return pltpu.make_async_remote_copy(
+            src_ref=x_buf.at[0, 0, 0],
+            dst_ref=x_buf.at[0, j, 0],
+            send_sem=x_send.at[0, j],
+            recv_sem=x_recv.at[0, j],
+            device_id={"tensor": peers[j]},
             device_id_type=MESH,
         )
 
@@ -350,6 +360,9 @@
         @pl.when(s > 0)
         def _():
             chain(c, 0).wait_recv()
+            if c == 0:
+                for j in range(1, tensors):
+                    spread_copy(j).start()
 
         fwd_copy(c, 0).start()
         absorb(c, 0, 0)
@@ -409,7 +422,7 @@
             )
             score[...] = score_part if step == 1 else score[...] + score_part
 
-        if step <= chunks - 2:
+        if step <= chunks - 1:
             multiply(c)
 
     mean_square = jnp.sum(squares[...], axis=1, keepdims=True) / (2 * tensors * width)
@@ -421,8 +434,7 @@
         for j in range(1, tensors):
             low_copy(j).start()
 
-    for c in order[max(chunks - 2, 0) :]:
-        multiply(c)
+    multiply(order[-1])
 
     wait_maps(*ups)
 
@@ -485,8 +497,9 @@
     @pl.when(s < last)
     def _():
         for c in order:
-            for j in range(1, tensors):
-                chain(c, j).start()
+            if c > 0:
+                for j in range(1, tensors):
+                    chain(c, j).start()
 
     @pl.when(s == last)
     def _():
@@ -522,6 +535,8 @@
 
     @pl.when(s > 0)
     def _():
+        for j in range(1, tensors):
+            spread_copy(j).wait_send()
         wait_maps_sent(*downs)
         for j, hh in pairs:
             if j or hh:
@@ -530,7 +545,7 @@
     @pl.when(s < last)
     def _():
         for c in range(chunks):
-            for j in range(tensors):
+            for j in range(tensors if c > 0 else 1):
                 chain(c, j).wait_send()
         for c in range(chunks):
             out_copy(c, 0).wait_recv()

time: 43.1 us -> 40 us (0.928)
  Pallas kernels: 41.6 us -> 38.4 us
    pallas_call x1, Pallas kernels: 41.6 us -> 38.4 us  [shards(): pl.pallas_call(functools.partial(kernel, sections, tensors), out_shape=ja...]
where the time goes in v4:
time: 40 us; the launch traced here: 39.9 us
  Pallas kernels  38.4 us (96%)
  local copies, waits for them, and re-layouts  1.42 us (4%)
    pallas_call x1, Pallas kernels, shards(): pl.pallas_call(functools.partial(kernel, sections, tensors), out_shape=ja...  38.4 us
    unnamed x1, local copies, waits for them, and re-layouts  1.42 us

profile of v4, /device:TPU:0, one launch (start us, length us, event | category | flops | bytes accessed | tf_op | source)
XLA Modules:
  0.0 39.9 jit_solution(1187582497598497083)
XLA Ops:
  0.0 38.4 %shard_map.73 = bf16[24,1024]{1,0:T(8,128)(2,1)} custom-call(bf16[48,1024]{1,0:T(8,128)(2,1)} %tokens_ref.1, f32[1,8192]{1,0:T(1,128)} %gain_ref.1, bf16[1,8192,1024]{2,1,0:T(8,128)(2,1)} %weight_ref.1, bf16[1,1,32,4096]{3,2,1,0:T(8,128)(2,1)} %down_ref.1, bf16[1,1,32,4096]{3,2,1,0:T(8,128)(2,1)} %up_ref.1, s32[1,48]{1,0:T(1,128)} %bitcast.2, s32[1,4]{1,0:T(1,128)} %bitcast.3), custom_call_target="tpu_custom_call" | custom-call | tf_op jit(solution)/shard_map/pallas_call | solution.py:566
  38.5 1.4 %copy.9 = bf16[24,1024]{1,0:T(8,128)(2,1)} copy(bf16[24,1024]{1,0:T(8,128)(2,1)} %shard_map.73) | data formatting | bytes 98304

commit v5 on v4

--- a/solution.py
+++ b/solution.py
@@ -293,8 +293,7 @@
     @pl.when(s > 0)
     def _():
         send_maps(*downs)
-
-    send_maps(*ups)
+        send_maps(*ups)
 
     row_copy.wait()
     slot_copy.wait()
@@ -392,6 +391,8 @@
     def _():
         down_copy.wait()
         down_remote.wait_recv()
+
+    pl.when(s == 0)(lambda: send_maps(*ups))
 
     for step in range(chunks + 1):
         if step < chunks:

time: 40 us -> 39.8 us (level)
  no operation moved by 1% of the time
where the time goes in v5:
time: 39.8 us; the launch traced here: 39.6 us
  Pallas kernels  38.2 us (96%)
  local copies, waits for them, and re-layouts  1.42 us (4%)
    pallas_call x1, Pallas kernels, shards(): pl.pallas_call(functools.partial(kernel, sections, tensors), out_shape=ja...  38.2 us
    unnamed x1, local copies, waits for them, and re-layouts  1.42 us

profile of v5, /device:TPU:0, one launch (start us, length us, event | category | flops | bytes accessed | tf_op | source)
XLA Modules:
  0.0 39.6 jit_solution(12881692662925225725)
XLA Ops:
  0.0 38.2 %shard_map.73 = bf16[24,1024]{1,0:T(8,128)(2,1)} custom-call(bf16[48,1024]{1,0:T(8,128)(2,1)} %tokens_ref.1, f32[1,8192]{1,0:T(1,128)} %gain_ref.1, bf16[1,8192,1024]{2,1,0:T(8,128)(2,1)} %weight_ref.1, bf16[1,1,32,4096]{3,2,1,0:T(8,128)(2,1)} %down_ref.1, bf16[1,1,32,4096]{3,2,1,0:T(8,128)(2,1)} %up_ref.1, s32[1,48]{1,0:T(1,128)} %bitcast.2, s32[1,4]{1,0:T(1,128)} %bitcast.3), custom_call_target="tpu_custom_call" | custom-call | tf_op jit(solution)/shard_map/pallas_call | solution.py:567
  38.2 1.4 %copy.9 = bf16[24,1024]{1,0:T(8,128)(2,1)} copy(bf16[24,1024]{1,0:T(8,128)(2,1)} %shard_map.73) | data formatting | bytes 98304
